TPU v7x, 32 devices: a whole 2x2x4 slice. The times are simulated.
32 devices in a mesh: prow: 4 (over x, core), pcol: 8 (over z, y).
Axes of the slice: x: 2, y: 2, z: 4, core: 2. Of those that a mesh axis runs over, the one named last changes fastest.
Arguments:
- trailing: float32 [2048, 2048], P('prow', 'pcol'), may hold values from -6 to 6
- panels: float32 [2048, 1024], P('prow', 'pcol'), may hold values from -0.1875 to 0.1875
- diag_inv: float32 [4, 256, 256], replicated, may hold values from -6 to 6
- ancestors: int32 [4, 4], replicated, may hold values from 0 to 7, as said below
- owner_map: int32 [8], replicated, may hold values from 0 to 7, each once
Outputs:
- inv_panel: float32 [2048, 1024], P(('prow', 'pcol'))
- inv_upper: float32 [1024, 2048], P('pcol', 'prow')
- inv_diag: float32 [4, 256, 256], replicated
Inputs may be any that keep to these rules, and one draw needn't show every extreme that they name: `ancestors`: each row names 4 distinct blocks; every block is named by exactly two siblings.
All inputs are finite; a program needn't handle non-finite values.
Results may differ from a plain program's by a relative error of at most 0.000071.
Values sent between devices are 32-bit elements; how exact they have to be, the bound alone decides.
A program may use at most 64 MiB of HBM per device.

v0:
```python
import jax
import jax.numpy as jnp
from jax import lax
from jax.sharding import PartitionSpec as P

NB = 256
SIBS = 4


def spread(array, axis, root):
    mine = lax.axis_index(axis) == root
    return lax.psum(jnp.where(mine, array, jnp.zeros_like(array)), axis)


def expand_cols(block_mask, ncols):
    siblings = jnp.arange(SIBS, dtype=jnp.int32)
    column_sib = jnp.arange(ncols, dtype=jnp.int32) // NB
    onehot = (column_sib[None, :] == siblings[:, None]).astype(jnp.float32)
    return jnp.dot(
        block_mask, onehot, precision=lax.Precision.HIGHEST, preferred_element_type=jnp.float32
    )


def shards(trailing, panels, diag_inv, ancestors, owner_map):
    row_index = lax.axis_index("prow")
    col_index = lax.axis_index("pcol")
    ncols_grid = lax.axis_size("pcol")
    nblk = owner_map.shape[0]
    rows_dev = trailing.shape[0]
    cols_dev = trailing.shape[1]
    row_blocks = rows_dev // NB
    col_blocks = cols_dev // NB
    part_rows = rows_dev // ncols_grid
    slots = owner_map[ancestors]
    member_t = (
        jnp.any(slots[:, :, None] == jnp.arange(nblk, dtype=jnp.int32)[None, None, :], axis=1)
        .astype(jnp.float32)
        .T
    )
    whole_rows = lax.all_gather(panels, "pcol", axis=1, tiled=True)
    mask_rows = lax.dynamic_slice_in_dim(member_t, row_index * row_blocks, row_blocks, 0)
    full_mask = jnp.repeat(expand_cols(mask_rows, whole_rows.shape[1]), NB, axis=0)
    masked_rows = whole_rows * full_mask
    first_col_block = col_index * col_blocks
    root = first_col_block // row_blocks
    offset = first_col_block % row_blocks * NB
    to_send = lax.dynamic_slice_in_dim(masked_rows, offset, cols_dev, 0)
    col_rows = spread(to_send, "prow", root)
    product = jnp.dot(
        trailing, col_rows, precision=lax.Precision.HIGHEST, preferred_element_type=jnp.float32
    )
    first_row = row_index * rows_dev + col_index * part_rows
    row_block = (first_row + jnp.arange(part_rows, dtype=jnp.int32)) // NB
    onehot_rows = (row_block[:, None] == jnp.arange(nblk, dtype=jnp.int32)[None, :]).astype(
        jnp.float32
    )
    row_member = jnp.dot(
        onehot_rows, member_t, precision=lax.Precision.HIGHEST, preferred_element_type=jnp.float32
    )
    reduced = lax.psum_scatter(product, "pcol", scatter_dimension=0, tiled=True)
    row_mask = jnp.repeat(row_member, NB, axis=1)
    inv_panel = -reduced * row_mask
    inv_upper = lax.all_to_all(inv_panel, "pcol", split_axis=1, concat_axis=0, tiled=True).T
    factor_rows = lax.dynamic_slice_in_dim(masked_rows, col_index * part_rows, part_rows, 0)
    term = -jnp.einsum(
        "rjn,rjm->jnm",
        factor_rows.reshape(part_rows, SIBS, NB),
        inv_panel.reshape(part_rows, SIBS, NB),
        precision=lax.Precision.HIGHEST,
    )
    inv_diag = diag_inv + lax.psum(term, ("prow", "pcol"))
    return (inv_panel, inv_upper, inv_diag)


def solution(mesh):
    placed = (P("prow", "pcol"), P("prow", "pcol"), P(), P(), P())
    return jax.shard_map(
        shards,
        mesh=mesh,
        in_specs=placed,
        out_specs=(P(("prow", "pcol"), None), P("pcol", "prow"), P()),
        check_vma=False,
    )
```

profile of v0, /device:TPU:19, one launch (start us, length us, event | category | flops | bytes accessed | tf_op | source)
XLA Modules:
  0.0 317.4 jit_solution(14911230518763129367)
XLA Ops:
  7.2 0.0 all-gather.2.cloned.1.call-start
  7.2 0.7 all-gather.2.cloned.1.call-update
  7.9 0.0 all-reduce.3.cloned.1.call-start
  8.0 0.7 compare_select_fusion
  8.7 0.1 reshape.60
  8.8 1.3 gather_fusion
  10.1 0.1 reshape.59
  10.2 0.1 fusion.6
  10.3 0.3 fusion.4
  10.5 50.4 %all-gather.2.cloned.1.call-done = f32[512,1024]{1,0:T(8,128)} async-done(((f32[512,128]{1,0:T(8,128)}), f32[512,1024]{1,0:T(8,128)}) %all-gather.2.cloned.1.call-update) | async-done | bytes 2097168 | tf_op jit(solution)/shard_map/all_gather | solution.py:40
  60.9 1.8 bitcast_multiply_fusion
  62.7 1.3 copy-done.1
  64.1 1.0 dynamic-slice_select_fusion
  65.1 0.0 all-reduce.3.cloned.1.call-update
  65.1 0.0 reduce-scatter.4.cloned.1.call-start
  65.2 35.0 %all-reduce.3.cloned.1.call-done = f32[256,1024]{1,0:T(8,128)} async-done(((f32[256,1024]{1,0:T(8,128)}), f32[256,1024]{1,0:T(8,128)}) %all-reduce.3.cloned.1.call-update) | async-done | bytes 1048592 | tf_op jit(solution)/shard_map/psum | solution.py:12
  100.2 4.7 %convolution_bitcast_fusion = f32[512,1024]{0,1:T(8,128)S(1)} fusion(f32[256,1024]{1,0:T(8,128)} %all-reduce.3.cloned.1.call-done, f32[512,256]{1,0:T(8,128)S(1)} %copy-done), kind=kOutput, calls=%fused_computation.2 | convolution fusion | flops 1610612736 | bytes 3670016 | tf_op jit(solution)/shard_map/dot_general | solution.py:49
  104.8 1.8 copy.41
  106.7 0.0 all-reduce.5.cloned.1.call-start
  106.8 0.2 fusion.2
  106.9 1.0 constant_dynamic-slice_fusion
  107.9 64.9 %reduce-scatter.4.cloned.1.call-done = f32[64,1024]{1,0:T(8,128)} async-done(((f32[512,1024]{1,0:T(8,128)}), f32[64,1024]{1,0:T(8,128)}) %reduce-scatter.4.cloned.1.call-update) | async-done | bytes 262160
  172.8 1.1 copy.42
  174.0 2.0 convolution_negate_fusion
  176.0 0.0 all-reduce.5.cloned.1.call-update
  176.0 0.9 copy.33
  176.9 5.1 %all-to-all-start = ((f32[64,8,128]{2,0,1:T(8,128)}), f32[64,8,128]{2,0,1:T(8,128)S(1)}, u32[]{:S(2)}, u32[]{:S(2)}) async-start(f32[64,8,128]{2,0,1:T(8,128)} %copy.33), calls=%async_computation | async-start | bytes 524288 | tf_op jit(solution)/shard_map/all_to_all | solution.py:63
  182.0 0.9 copy.36
  182.9 4.1 %all-to-all-done = f32[64,8,128]{2,0,1:T(8,128)S(1)} async-done(((f32[64,8,128]{2,0,1:T(8,128)}), f32[64,8,128]{2,0,1:T(8,128)S(1)}, u32[]{:S(2)}, u32[]{:S(2)}) %all-to-all-start) | async-done | bytes 262176 | tf_op jit(solution)/shard_map/all_to_all | solution.py:63
  187.0 0.8 copy.37
  187.8 120.7 %all-reduce.5.cloned.1.call-done = f32[4,256,256]{2,1,0:T(8,128)} async-done(((f32[4,256,256]{2,1,0:T(8,128)}), f32[4,256,256]{2,1,0:T(8,128)}) %all-reduce.5.cloned.1.call-update) | async-done | bytes 1048592 | tf_op jit(solution)/shard_map/psum | solution.py:71
  308.6 2.3 add.57
  (10 shorter events, 0.1 us)
Async XLA Ops:
  7.2 93.0 %copy-start = (f32[512,256]{1,0:T(8,128)S(1)}, f32[512,256]{1,0:T(8,128)}, u32[]{:S(2)}) copy-start(f32[512,256]{1,0:T(8,128)} %param.5) | copy-start | bytes 1572868
  7.2 53.7 %all-gather.2.cloned.1.call-start = ((), (), s32[]{:S(2)}) async-start(), calls=%async_computation.2 | async-start | bytes 2359296 | tf_op jit(solution)/shard_map/all_gather | solution.py:40
  7.9 92.3 %all-reduce.3.cloned.1.call-start = ((), (), s32[]{:S(2)}) async-start(), calls=%async_computation.3 | async-start | bytes 2097152 | tf_op jit(solution)/shard_map/psum | solution.py:12
  62.7 1.3 copy-start.1
  65.1 107.7 %reduce-scatter.4.cloned.1.call-start = ((), (), s32[]{:S(2)}) async-start(), calls=%async_computation.5 | async-start | bytes 2359296
  106.7 201.9 %all-reduce.5.cloned.1.call-start = ((), (), s32[]{:S(2)}) async-start(), calls=%async_computation.4 | async-start | bytes 2097152 | tf_op jit(solution)/shard_map/psum | solution.py:71
  176.0 132.6 %copy-start.2 = (f32[4,256,256]{2,1,0:T(8,128)S(1)}, f32[4,256,256]{2,1,0:T(8,128)}, u32[]{:S(2)}) copy-start(f32[4,256,256]{2,1,0:T(8,128)} %param.7) | copy-start | bytes 3145732
  176.9 10.1 %all-to-all-start = ((f32[64,8,128]{2,0,1:T(8,128)}), f32[64,8,128]{2,0,1:T(8,128)S(1)}, u32[]{:S(2)}, u32[]{:S(2)}) async-start(f32[64,8,128]{2,0,1:T(8,128)} %copy.33), calls=%async_computation | async-start | bytes 524288 | tf_op jit(solution)/shard_map/all_to_all | solution.py:63
Sparse Core Ops, SparseCore 0:
  10.1 50.8 all-gather.1
  65.3 34.8 all-reduce.2
  106.8 65.9 reduce-scatter.3
  179.2 129.2 all-reduce.4
where the time goes:
time: 322 us; the launch traced here: 317 us
  waiting for transfers between devices  276 us (86%)
  between operations  13.9 us (4%)
  local copies, waits for them, and re-layouts  9.38 us (3%)
  matrix products  7.11 us (2%)
  other arithmetic  6.01 us (2%)
  starting transfers between devices  5.23 us (2%)
    psum x1, waiting for transfers between devices, shards(): inv_diag = diag_inv + lax.psum(term, ('prow', 'pcol'))  121 us
    unnamed x5, waiting for transfers between devices  65.6 us
    all_gather x1, waiting for transfers between devices, shards(): whole_rows = lax.all_gather(panels, 'pcol', axis=1, tiled=True)  50.4 us
    psum x1, waiting for transfers between devices, spread(): return lax.psum(jnp.where(mine, array, jnp.zeros_like(array)), axis)  35 us
  transfers between devices with their start and end apart: 5, of which 5 were waited for; matrix products, arithmetic and copies ran while one was open for 2% of the time, Pallas kernels for 0%

commit v1 on v0

v1 whole, which is shorter than its diff:
```python
import functools

import jax
import jax.numpy as jnp
from jax import lax
from jax.experimental import pallas as pl
from jax.experimental.pallas import tpu as pltpu
from jax.sharding import PartitionSpec as P

NB = 256
SIBS = 4
SHARE = 2
F32 = jnp.float32
BF16 = jnp.bfloat16


def split(value):
    high = value.astype(BF16)
    return high, (value - high.astype(F32)).astype(BF16)


def dot3(a, b):
    a_high, a_low = a
    b_high, b_low = b
    dot = functools.partial(jnp.dot, preferred_element_type=F32)
    return dot(a_high, b_high) + (dot(a_high, b_low) + dot(a_low, b_high))


def kernel(
    R, C, an, om, t_ref, p_ref, panel_ref, upper_ref, diag_ref,
    pg, grp, mt, b_ref, y, yr, zr, stage, u, d_ref, rr,
    a1_s, a1_r, g_s, g_r, a2_s, a2_r, a2f_s, a2f_r, y_s, y_r, z_s, z_r,
    u_s, u_r, d_s, d_r, ez_s, ez_r, ey_s, ey_r, ex_s, ex_r, ec_s, ec_r,
):
    r = lax.axis_index("prow")
    c = lax.axis_index("pcol")
    rows, cols = t_ref.shape
    width = p_ref.shape[1]
    ratio = rows // cols
    quarter = cols // R
    part = rows // C
    group = NB // width
    half = C // 2
    pairs = R // 2
    chunk = NB // R
    par = lax.rem(c, 2)
    other_c = c + 1 - 2 * par
    rpar = lax.rem(r, 2)
    other_r = r + 1 - 2 * rpar
    sends = []

    def copy(src, dst, ssem, rsem, to_r, to_c):
        return pltpu.make_async_remote_copy(
            src_ref=src, dst_ref=dst, send_sem=ssem, recv_sem=rsem,
            device_id=(to_r, to_c), device_id_type=pl.DeviceIdType.MESH,
        )

    def send(*args):
        op = copy(*args)
        op.start()
        sends.append(op)

    def arrived(dst, ssem, rsem):
        copy(dst, dst, ssem, rsem, other_r, c).wait_recv()

    def same_parity(index, count, step):
        return lax.rem(index // 2 + step, count) * 2 + lax.rem(index, 2)

    own = []
    for step in [*range(1, R), 0]:
        k = lax.rem(r + step, R)
        for b in range(ratio):
            dest = r * ratio + b
            piece = p_ref.at[pl.ds(pl.multiple_of(b * cols + k * quarter, quarter), quarter)]
            args = (piece, pg.at[k, c], a1_s.at[b, step], a1_r.at[c], k, dest)
            if step:
                send(*args)
            else:
                own.append((dest, args))
    for dest, args in own:
        @pl.when(dest != c)
        def _():
            copy(*args).start()

        @pl.when(dest == c)
        def _():
            pg[r, c] = args[0][...]

    base = (c // group) * group
    member = c - base
    for step in range(1, group):
        to = base + lax.rem(member + step, group)
        send(p_ref, grp.at[member], g_s.at[step - 1], g_r.at[step - 1], r, to)
    grp[member] = p_ref[...]

    slots = [[om[an[j, a]] for a in range(an.shape[1])] for j in range(SIBS)]

    def members(s):
        found = []
        for j in range(SIBS):
            flag = jnp.int32(0)
            for slot in slots[j]:
                flag = flag | jnp.where(slot == s, 1, 0).astype(jnp.int32)
            found.append(flag)
        return found

    def places(s):
        flags, before = members(s), jnp.int32(0)
        out = [[] for _ in range(SHARE)]
        for flag in flags:
            for k in range(SHARE):
                out[k].append((flag * jnp.where(before == k, 1, 0).astype(jnp.int32)).astype(F32))
            before = before + flag
        return out

    row_blocks = rows // NB
    row_places = [places(r * row_blocks + b) for b in range(row_blocks)]
    my_place = places((r * rows + c * part) // NB)
    col_flags = [flag.astype(F32) for flag in members(c)]

    root = c // ratio
    for step in range(SIBS):
        j = lax.rem(c // group + step, SIBS)
        for i in range(group):
            source = j * group + i
            @pl.when(jnp.logical_not((root == r) & (source == c)))
            def _():
                arrived(pg.at[r, source], a1_s.at[0, 0], a1_r.at[source])
        block = pg.at[r, pl.ds(j * group, group)]
        for to in range(1, pairs):
            send(block, block, a2_s.at[to, step], a2_r.at[to, j], same_parity(r, pairs, to), c)
        send(block, block, a2_s.at[0, step], a2_r.at[0, j], other_r, c)
    for step in range(SIBS):
        for to in range(1, pairs):
            j = lax.rem(c // group + step, SIBS)
            source = same_parity(r, pairs, pairs - to)
            block = pg.at[source, pl.ds(j * group, group)]
            arrived(block, a2_s.at[to, step], a2_r.at[to, j])
            send(block, block, a2f_s.at[to - 1, step], a2f_r.at[to - 1, j], other_r, c)
    for j in range(SIBS):
        arrived(pg.at[other_r, pl.ds(j * group, group)], a2_s.at[0, j], a2_r.at[0, j])
        for to in range(1, pairs):
            source = same_parity(other_r, pairs, pairs - to)
            block = pg.at[source, pl.ds(j * group, group)]
            arrived(block, a2f_s.at[to - 1, j], a2f_r.at[to - 1, j])

    for s in range(row_blocks):
        for k in range(SHARE):
            scale = [row_places[s][k][j] * col_flags[j] for j in range(SIBS)]
            for q in range(R):
                for i in range(group):
                    total = scale[0] * pg[q, i]
                    for j in range(1, SIBS):
                        total = total + scale[j] * pg[q, j * group + i]
                    b_ref[s, q * quarter:(q + 1) * quarter,
                          k * NB + i * width:k * NB + (i + 1) * width] = total
        y[s * NB:(s + 1) * NB, :] = dot3(split(t_ref[s * NB:(s + 1) * NB, :]), split(b_ref[s]))
        for i in range(s * NB // (2 * part), (s + 1) * NB // (2 * part)):
            piece = y.at[pl.ds(pl.multiple_of((2 * i + 1 - par) * part, part), part)]
            send(piece, yr.at[i], y_s.at[i], y_r.at[i], r, other_c)

    for step in [*range(1, half), 0]:
        i = lax.rem(c // 2 + step, half)
        place = pl.ds(pl.multiple_of((2 * i + par) * part, part), part)
        arrived(yr.at[i], y_s.at[i], y_r.at[i])
        y[place, :] = y[place, :] + yr[i]
        if step:
            send(y.at[place], zr.at[step - 1], z_s.at[step - 1], z_r.at[step - 1], r, 2 * i + par)

    for step in range(1, group):
        source = base + lax.rem(member + group - step, group)
        arrived(grp.at[source - base], g_s.at[step - 1], g_r.at[step - 1])
    for i in range(group):
        mt[i * width:(i + 1) * width, :] = grp[i].T
    mt_split = split(mt[...])

    total = y[pl.ds(pl.multiple_of(c * part, part), part), :]
    for step in range(1, half):
        arrived(zr.at[step - 1], z_s.at[step - 1], z_r.at[step - 1])
        total = total + zr[step - 1]
    for j in range(SIBS):
        block = -(my_place[0][j] * total[:, :NB] + my_place[1][j] * total[:, NB:])
        panel_ref[:, j * NB:(j + 1) * NB] = block
        for i in range(group):
            stage[j * group + i] = block[:, i * width:(i + 1) * width]

    for step in range(1, C):
        to = lax.rem(c + step, C)
        send(stage.at[to], u.at[c], u_s.at[step - 1], u_r.at[step - 1], r, to)
    u[c] = stage[c]
    for step in range(1, C):
        source = lax.rem(c + C - step, C)
        arrived(u.at[source], u_s.at[step - 1], u_r.at[step - 1])
    x = u[...].reshape(rows, width)
    upper_ref[...] = x.T

    d_ref[...] = dot3(mt_split, split(x))
    for step in range(1, R):
        to = lax.rem(r + step, R)
        piece = d_ref.at[pl.ds(pl.multiple_of(to * chunk, chunk), chunk)]
        send(piece, rr.at[step - 1], d_s.at[step - 1], d_r.at[step - 1], to, c)
    total = d_ref[pl.ds(pl.multiple_of(r * chunk, chunk), chunk), :]
    for step in range(1, R):
        arrived(rr.at[step - 1], d_s.at[step - 1], d_r.at[step - 1])
        total = total + rr[step - 1]
    place = c // 2
    diag_ref[par, r, place] = total
    mine = diag_ref.at[par, r, place]
    for step in range(1, half):
        to = lax.rem(place + step, half)
        send(mine, mine, ez_s.at[step - 1], ez_r.at[step - 1], r, 2 * to + par)
    for step in range(1, half):
        source = lax.rem(place + half - step, half)
        arrived(diag_ref.at[par, r, source], ez_s.at[step - 1], ez_r.at[step - 1])

    def spread(which, block):
        for to in range(1, pairs):
            send(block, block, ex_s.at[which, to], ex_r.at[which, to], same_parity(r, pairs, to), c)
        send(block, block, ec_s.at[which, 0], ec_r.at[which, 0], other_r, c)

    block = diag_ref.at[par, r]
    send(block, block, ey_s.at[0], ey_r.at[0], r, other_c)
    spread(0, block)
    block = diag_ref.at[1 - par, r]
    arrived(block, ey_s.at[0], ey_r.at[0])
    spread(1, block)
    for which in range(2):
        side = par if which == 0 else 1 - par
        for to in range(1, pairs):
            block = diag_ref.at[side, same_parity(r, pairs, pairs - to)]
            arrived(block, ex_s.at[which, to], ex_r.at[which, to])
            send(block, block, ec_s.at[which, to], ec_r.at[which, to], other_r, c)
    for which in range(2):
        side = par if which == 0 else 1 - par
        for to in range(pairs):
            block = diag_ref.at[side, same_parity(other_r, pairs, (pairs - to) % pairs)]
            arrived(block, ec_s.at[which, to], ec_r.at[which, to])

    for op in sends:
        op.wait_send()
    for dest, args in own:
        @pl.when(dest != c)
        def _():
            copy(*args).wait_send()


def shards(R, C, trailing, panels, diag_inv, ancestors, owner_map):
    rows, cols = trailing.shape
    width = panels.shape[1]
    ratio = rows // cols
    part = rows // C
    group = NB // width
    half = C // 2
    pairs = R // 2
    chunk = NB // R
    wide = SHARE * NB
    dma = pltpu.SemaphoreType.DMA
    sems = []
    for shape in (
        (ratio, R), (C,), (max(group - 1, 1),), (max(group - 1, 1),),
        (pairs, SIBS), (pairs, SIBS), (max(pairs - 1, 1), SIBS), (max(pairs - 1, 1), SIBS),
        (half,), (half,), (half - 1,), (half - 1,), (C - 1,), (C - 1,),
        (R - 1,), (R - 1,), (half - 1,), (half - 1,), (1,), (1,),
        (2, pairs), (2, pairs), (2, pairs), (2, pairs),
    ):
        sems.append(dma(shape))
    vmem = pl.BlockSpec(memory_space=pltpu.VMEM)
    smem = pl.BlockSpec(memory_space=pltpu.SMEM)
    inv_panel, inv_upper, term = pl.pallas_call(
        functools.partial(kernel, R, C),
        out_shape=(
            jax.ShapeDtypeStruct((part, SIBS * NB), F32),
            jax.ShapeDtypeStruct((width, rows), F32),
            jax.ShapeDtypeStruct((2, R, half, chunk, width), F32),
        ),
        in_specs=[smem, smem, vmem, vmem],
        out_specs=(vmem, vmem, vmem),
        scratch_shapes=[
            pltpu.VMEM((R, C, cols // R, width), F32),
            pltpu.VMEM((group, rows, width), F32),
            pltpu.VMEM((NB, rows), F32),
            pltpu.VMEM((rows // NB, cols, wide), F32),
            pltpu.VMEM((rows, wide), F32),
            pltpu.VMEM((half, part, wide), F32),
            pltpu.VMEM((half - 1, part, wide), F32),
            pltpu.VMEM((C, part, width), F32),
            pltpu.VMEM((C, part, width), F32),
            pltpu.VMEM((NB, width), F32),
            pltpu.VMEM((R - 1, chunk, width), F32),
            *sems,
        ],
        compiler_params=pltpu.CompilerParams(
            has_side_effects=True, vmem_limit_bytes=40 * 1024 * 1024
        ),
    )(ancestors, owner_map, trailing, panels)
    term = term.reshape(2, R, SIBS, group // 2, chunk, width)
    term = term.transpose(2, 1, 4, 3, 0, 5).reshape(SIBS, NB, NB)
    return inv_panel, inv_upper, diag_inv - term


def solution(mesh):
    placed = (P("prow", "pcol"), P("prow", "pcol"), P(), P(), P())
    return jax.shard_map(
        functools.partial(shards, mesh.shape["prow"], mesh.shape["pcol"]),
        mesh=mesh,
        in_specs=placed,
        out_specs=(P(("prow", "pcol"), None), P("pcol", "prow"), P()),
        check_vma=False,
    )
```

time: 322 us -> 86.1 us (0.27); the launches traced: 317 us -> 85.2 us
  waiting for transfers between devices: 276 us -> 0 us
  Pallas kernels: 0 us -> 75.9 us
  between operations: 13.9 us -> 0.67 us
  matrix products: 7.11 us -> 0 us
  starting transfers between devices: 5.23 us -> 0 us
  other arithmetic: 6.01 us -> 2.33 us
    psum x2 -> x0, waiting for transfers between devices: 156 us -> none  [the longest x1 121 us: shards(): inv_diag = diag_inv + lax.psum(term, ('prow', 'pcol'))]
    pallas_call x0 -> x1, Pallas kernels: none -> 75.9 us  [shards(): pl.pallas_call(functools.partial(kernel, R, C), out_shape=(jax.ShapeDtype...]
    unnamed x5 -> x0, waiting for transfers between devices: 65.6 us -> none
    all_gather x1 -> x0, waiting for transfers between devices: 50.4 us -> none  [shards(): whole_rows = lax.all_gather(panels, 'pcol', axis=1, tiled=True)]
    dot_general x4 -> x0, matrix products: 7.11 us -> none  [the longest x1 4.65 us: shards(): jnp.dot(trailing, col_rows, precision=lax.Precision.HIGHEST, preferred_el...]
    all_to_all x1 -> x0, starting transfers between devices: 5.07 us -> none  [shards(): lax.all_to_all(inv_panel, 'pcol', split_axis=1, concat_axis=0, tiled=True)]
    all_to_all x1 -> x0, waiting for transfers between devices: 4.11 us -> none  [shards(): lax.all_to_all(inv_panel, 'pcol', split_axis=1, concat_axis=0, tiled=True)]
  transfers between devices with their start and end apart: 5 -> 0, of which waited for: 5 -> 0; matrix products, arithmetic and copies ran while one was open for 2% -> 0% of each run, Pallas kernels for 0% -> 0%
where the time goes in v1:
time: 86.1 us; the launch traced here: 85.2 us
  Pallas kernels  75.9 us (88%)
  local copies, waits for them, and re-layouts  6.38 us (7%)
  other arithmetic  2.33 us (3%)
    pallas_call x1, Pallas kernels, shards(): pl.pallas_call(functools.partial(kernel, R, C), out_shape=(jax.ShapeDtype...  75.9 us
    unnamed x10, local copies, waits for them, and re-layouts  4.72 us
    sub x1, other arithmetic, shards(): return (inv_panel, inv_upper, diag_inv - term)  2.33 us

profile of v1, /device:TPU:19, one launch (start us, length us, event | category | flops | bytes accessed | tf_op | source)
XLA Modules:
  0.0 85.2 jit_solution(1486952150142919122)
XLA Ops:
  0.6 0.0 copy-start
  0.6 1.0 %copy-done = f32[512,256]{1,0:T(8,128)S(1)} copy-done((f32[512,256]{1,0:T(8,128)S(1)}, f32[512,256]{1,0:T(8,128)}, u32[]{:S(2)}) %copy-start) | copy-done | bytes 524312
  1.7 0.0 copy-start.1
  1.7 0.9 %copy-done.1 = f32[512,128]{1,0:T(8,128)S(1)} copy-done((f32[512,128]{1,0:T(8,128)S(1)}, f32[512,128]{1,0:T(8,128)}, u32[]{:S(2)}) %copy-start.1) | copy-done | bytes 262168
  2.6 0.0 copy-start.2
  2.6 0.7 copy-done.2
  3.3 0.0 copy-start.3
  3.3 0.7 copy-done.3
  4.0 75.9 %shard_map.76 = (f32[64,1024]{1,0:T(8,128)S(1)}, f32[128,512]{1,0:T(8,128)S(1)}, f32[2,4,4,64,128]{4,3,2,1,0:T(8,128)S(1)}) custom-call(s32[4,4]{1,0:T(4,128)S(1)} %copy-done.2, s32[8]{0:T(128)S(1)} %copy-done.3, f32[512,256]{1,0:T(8,128)S(1)} %copy-done, f32[512,128]{1,0:T(8,128)S(1)} %copy-done.1), custom_call_target="tpu_custom_call" | custom-call | tf_op jit(solution)/shard_map/pallas_call | solution.py:269
  79.8 0.8 copy.8
  80.7 0.8 reshape.13
  81.5 2.3 %sub.3 = f32[4,256,256]{2,1,0:T(8,128)} subtract(f32[4,256,256]{2,1,0:T(8,128)} %param.7, f32[4,256,256]{2,1,0:T(8,128)S(1)} %reshape.13) | non-fusion elementwise | flops 262144 | bytes 3145728 | tf_op jit(solution)/shard_map/sub | solution.py:298
  83.8 0.7 copy.11
  84.5 0.7 copy.12
Async XLA Ops:
  0.6 1.0 %copy-start = (f32[512,256]{1,0:T(8,128)S(1)}, f32[512,256]{1,0:T(8,128)}, u32[]{:S(2)}) copy-start(f32[512,256]{1,0:T(8,128)} %t_ref.1) | copy-start | bytes 1572868
  1.7 0.9 %copy-start.1 = (f32[512,128]{1,0:T(8,128)S(1)}, f32[512,128]{1,0:T(8,128)}, u32[]{:S(2)}) copy-start(f32[512,128]{1,0:T(8,128)} %p_ref.1) | copy-start | bytes 786436
  2.6 0.7 copy-start.2
  3.3 0.7 copy-start.3

commit v2 on v1

--- a/solution.py
+++ b/solution.py
@@ -27,9 +27,10 @@
 
 
 def kernel(
-    R, C, an, om, t_ref, p_ref, panel_ref, upper_ref, diag_ref,
-    pg, grp, mt, b_ref, y, yr, zr, stage, u, d_ref, rr,
-    a1_s, a1_r, g_s, g_r, a2_s, a2_r, a2f_s, a2f_r, y_s, y_r, z_s, z_r,
+    R, C, an_hbm, om_hbm, t_hbm, p_ref, inv_hbm, panel_ref, upper_ref, diag_ref,
+    an, om, t_ref, inv_ref, t_high, t_low,
+    pg, grp, mt, b_ref, y, yr, zr, stage, u, d_ref, rr, eg,
+    load, a1_s, a1_r, g_s, g_r, a2_s, a2_r, a2f_s, a2f_r, y_s, y_r, z_s, z_r,
     u_s, u_r, d_s, d_r, ez_s, ez_r, ey_s, ey_r, ex_s, ex_r, ec_s, ec_r,
 ):
     r = lax.axis_index("prow")
@@ -63,35 +64,54 @@
     def arrived(dst, ssem, rsem):
         copy(dst, dst, ssem, rsem, other_r, c).wait_recv()
 
+    def flip(index, bits):
+        bit = 1
+        out = index
+        while bit <= bits:
+            if bits & bit:
+                out = out + bit * (1 - 2 * lax.rem(index // bit, 2))
+            bit *= 2
+        return out
+
     def same_parity(index, count, step):
         return lax.rem(index // 2 + step, count) * 2 + lax.rem(index, 2)
+
+    loads = [
+        pltpu.make_async_copy(src, dst, load.at[n])
+        for n, (src, dst) in enumerate(
+            ((p_ref, grp.at[lax.rem(c, group)]), (an_hbm, an), (om_hbm, om), (t_hbm, t_ref),
+             (inv_hbm, inv_ref))
+        )
+    ]
+    for op in loads:
+        op.start()
 
     own = []
     for step in [*range(1, R), 0]:
         k = lax.rem(r + step, R)
         for b in range(ratio):
             dest = r * ratio + b
-            piece = p_ref.at[pl.ds(pl.multiple_of(b * cols + k * quarter, quarter), quarter)]
+            span = pl.ds(pl.multiple_of(b * cols + k * quarter, quarter), quarter)
+            piece = p_ref.at[span]
             args = (piece, pg.at[k, c], a1_s.at[b, step], a1_r.at[c], k, dest)
             if step:
                 send(*args)
             else:
-                own.append((dest, args))
-    for dest, args in own:
+                own.append((dest, args, span))
+    base = (c // group) * group
+    member = c - base
+    for dest, args, span in own:
         @pl.when(dest != c)
         def _():
             copy(*args).start()
-
+    loads[0].wait()
+    for dest, args, span in own:
         @pl.when(dest == c)
         def _():
-            pg[r, c] = args[0][...]
-
-    base = (c // group) * group
-    member = c - base
-    for step in range(1, group):
-        to = base + lax.rem(member + step, group)
-        send(p_ref, grp.at[member], g_s.at[step - 1], g_r.at[step - 1], r, to)
-    grp[member] = p_ref[...]
+            pg[r, c] = grp[member, span, :]
+    for op in loads[1:4]:
+        op.wait()
+    t_high[...], t_low[...] = split(t_ref[...])
 
     slots = [[om[an[j, a]] for a in range(an.shape[1])] for j in range(SIBS)]
 
@@ -130,6 +150,9 @@
         for to in range(1, pairs):
             send(block, block, a2_s.at[to, step], a2_r.at[to, j], same_parity(r, pairs, to), c)
         send(block, block, a2_s.at[0, step], a2_r.at[0, j], other_r, c)
+    for step in range(1, group):
+        to = base + lax.rem(member + step, group)
+        send(p_ref, grp.at[member], g_s.at[step - 1], g_r.at[step - 1], r, to)
     for step in range(SIBS):
         for to in range(1, pairs):
             j = lax.rem(c // group + step, SIBS)
@@ -154,13 +177,14 @@
                         total = total + scale[j] * pg[q, j * group + i]
                     b_ref[s, q * quarter:(q + 1) * quarter,
                           k * NB + i * width:k * NB + (i + 1) * width] = total
-        y[s * NB:(s + 1) * NB, :] = dot3(split(t_ref[s * NB:(s + 1) * NB, :]), split(b_ref[s]))
-        for i in range(s * NB // (2 * part), (s + 1) * NB // (2 * part)):
-            piece = y.at[pl.ds(pl.multiple_of((2 * i + 1 - par) * part, part), part)]
-            send(piece, yr.at[i], y_s.at[i], y_r.at[i], r, other_c)
-
-    for step in [*range(1, half), 0]:
-        i = lax.rem(c // 2 + step, half)
+        here = slice(s * NB, (s + 1) * NB)
+        y[here, :] = dot3((t_high[here, :], t_low[here, :]), split(b_ref[s]))
+
+    order = [flip(c // 2, step) for step in (*range(half - 1, 0, -1), 0)]
+    for i in order:
+        piece = y.at[pl.ds(pl.multiple_of((2 * i + 1 - par) * part, part), part)]
+        send(piece, yr.at[i], y_s.at[i], y_r.at[i], r, other_c)
+    for step, i in zip((*range(half - 1, 0, -1), 0), order):
         place = pl.ds(pl.multiple_of((2 * i + par) * part, part), part)
         arrived(yr.at[i], y_s.at[i], y_r.at[i])
         y[place, :] = y[place, :] + yr[i]
@@ -204,41 +228,62 @@
         arrived(rr.at[step - 1], d_s.at[step - 1], d_r.at[step - 1])
         total = total + rr[step - 1]
     place = c // 2
-    diag_ref[par, r, place] = total
-    mine = diag_ref.at[par, r, place]
-    for step in range(1, half):
-        to = lax.rem(place + step, half)
+    eg[par, r, place] = total
+
+    def spread(which, step, side, at, over_pair):
+        block = eg.at[side, r, at]
+        if over_pair:
+            send(block, block, ey_s.at[step], ey_r.at[step], r, other_c)
+        for to in range(1, pairs):
+            send(block, block, ex_s.at[which, to, step], ex_r.at[which, to, step],
+                 same_parity(r, pairs, to), c)
+        send(block, block, ec_s.at[which, 0, step], ec_r.at[which, 0, step], other_r, c)
+
+    def onward(which, step, side, at):
+        for to in range(1, pairs):
+            block = eg.at[side, same_parity(r, pairs, pairs - to), at]
+            arrived(block, ex_s.at[which, to, step], ex_r.at[which, to, step])
+            send(block, block, ec_s.at[which, to, step], ec_r.at[which, to, step], other_r, c)
+
+    mine = eg.at[par, r, place]
+    for step in range(half - 1, 0, -1):
+        to = flip(place, step)
         send(mine, mine, ez_s.at[step - 1], ez_r.at[step - 1], r, 2 * to + par)
-    for step in range(1, half):
-        source = lax.rem(place + half - step, half)
-        arrived(diag_ref.at[par, r, source], ez_s.at[step - 1], ez_r.at[step - 1])
-
-    def spread(which, block):
-        for to in range(1, pairs):
-            send(block, block, ex_s.at[which, to], ex_r.at[which, to], same_parity(r, pairs, to), c)
-        send(block, block, ec_s.at[which, 0], ec_r.at[which, 0], other_r, c)
-
-    block = diag_ref.at[par, r]
-    send(block, block, ey_s.at[0], ey_r.at[0], r, other_c)
-    spread(0, block)
-    block = diag_ref.at[1 - par, r]
-    arrived(block, ey_s.at[0], ey_r.at[0])
-    spread(1, block)
+    spread(0, 0, par, place, True)
+    events = [(0, 1), (1, 0)]
+    for step in range(2, half):
+        events += [(0, step), (1, step - 1)]
+    events.append((1, half - 1))
+    before = (0, 0)
+    for which, step in events:
+        at = flip(place, step)
+        if which == 0:
+            arrived(eg.at[par, r, at], ez_s.at[step - 1], ez_r.at[step - 1])
+            spread(0, step, par, at, True)
+        else:
+            arrived(eg.at[1 - par, r, at], ey_s.at[step], ey_r.at[step])
+            spread(1, step, 1 - par, at, False)
+        side = par if before[0] == 0 else 1 - par
+        onward(*before, side, flip(place, before[1]))
+        before = (which, step)
+    onward(*before, par if before[0] == 0 else 1 - par, flip(place, before[1]))
+    loads[4].wait()
     for which in range(2):
         side = par if which == 0 else 1 - par
-        for to in range(1, pairs):
-            block = diag_ref.at[side, same_parity(r, pairs, pairs - to)]
-            arrived(block, ex_s.at[which, to], ex_r.at[which, to])
-            send(block, block, ec_s.at[which, to], ec_r.at[which, to], other_r, c)
-    for which in range(2):
-        side = par if which == 0 else 1 - par
-        for to in range(pairs):
-            block = diag_ref.at[side, same_parity(other_r, pairs, (pairs - to) % pairs)]
-            arrived(block, ec_s.at[which, to], ec_r.at[which, to])
+        for step in range(half):
+            for to in range(pairs):
+                block = eg.at[side, same_parity(other_r, pairs, (pairs - to) % pairs), flip(place, step)]
+                arrived(block, ec_s.at[which, to, step], ec_r.at[which, to, step])
+    for column in range(C):
+        j, i = column // group, column % group
+        lanes = slice(i * width, (i + 1) * width)
+        for k in range(R):
+            span = slice(k * chunk, (k + 1) * chunk)
+            diag_ref[j, span, lanes] = inv_ref[j, span, lanes] - eg[column % 2, k, column // 2]
 
     for op in sends:
         op.wait_send()
-    for dest, args in own:
+    for dest, args, span in own:
         @pl.when(dest != c)
         def _():
             copy(*args).wait_send()
@@ -255,27 +300,33 @@
     chunk = NB // R
     wide = SHARE * NB
     dma = pltpu.SemaphoreType.DMA
-    sems = []
+    sems = [dma((5,))]
     for shape in (
         (ratio, R), (C,), (max(group - 1, 1),), (max(group - 1, 1),),
         (pairs, SIBS), (pairs, SIBS), (max(pairs - 1, 1), SIBS), (max(pairs - 1, 1), SIBS),
         (half,), (half,), (half - 1,), (half - 1,), (C - 1,), (C - 1,),
-        (R - 1,), (R - 1,), (half - 1,), (half - 1,), (1,), (1,),
-        (2, pairs), (2, pairs), (2, pairs), (2, pairs),
+        (R - 1,), (R - 1,), (half - 1,), (half - 1,), (half,), (half,),
+        (2, pairs, half), (2, pairs, half), (2, pairs, half), (2, pairs, half),
     ):
         sems.append(dma(shape))
     vmem = pl.BlockSpec(memory_space=pltpu.VMEM)
-    smem = pl.BlockSpec(memory_space=pltpu.SMEM)
-    inv_panel, inv_upper, term = pl.pallas_call(
+    anywhere = pl.BlockSpec(memory_space=pl.ANY)
+    return pl.pallas_call(
         functools.partial(kernel, R, C),
         out_shape=(
             jax.ShapeDtypeStruct((part, SIBS * NB), F32),
             jax.ShapeDtypeStruct((width, rows), F32),
-            jax.ShapeDtypeStruct((2, R, half, chunk, width), F32),
+            jax.ShapeDtypeStruct(diag_inv.shape, F32),
         ),
-        in_specs=[smem, smem, vmem, vmem],
+        in_specs=[anywhere] * 5,
         out_specs=(vmem, vmem, vmem),
         scratch_shapes=[
+            pltpu.SMEM(ancestors.shape, jnp.int32),
+            pltpu.SMEM(owner_map.shape, jnp.int32),
+            pltpu.VMEM(trailing.shape, F32),
+            pltpu.VMEM(diag_inv.shape, F32),
+            pltpu.VMEM(trailing.shape, BF16),
+            pltpu.VMEM(trailing.shape, BF16),
             pltpu.VMEM((R, C, cols // R, width), F32),
             pltpu.VMEM((group, rows, width), F32),
             pltpu.VMEM((NB, rows), F32),
@@ -287,15 +338,13 @@
             pltpu.VMEM((C, part, width), F32),
             pltpu.VMEM((NB, width), F32),
             pltpu.VMEM((R - 1, chunk, width), F32),
+            pltpu.VMEM((2, R, half, chunk, width), F32),
             *sems,
         ],
         compiler_params=pltpu.CompilerParams(
-            has_side_effects=True, vmem_limit_bytes=40 * 1024 * 1024
+            has_side_effects=True, vmem_limit_bytes=56 * 1024 * 1024
         ),
-    )(ancestors, owner_map, trailing, panels)
-    term = term.reshape(2, R, SIBS, group // 2, chunk, width)
-    term = term.transpose(2, 1, 4, 3, 0, 5).reshape(SIBS, NB, NB)
-    return inv_panel, inv_upper, diag_inv - term
+    )(ancestors, owner_map, trailing, panels, diag_inv)
 
 
 def solution(mesh):

time: 86.1 us -> 80.1 us (0.930)
  other arithmetic: 2.33 us -> 0 us
  local copies, waits for them, and re-layouts: 6.38 us -> 4.4 us
  Pallas kernels: 75.9 us -> 74.9 us
    sub x1 -> x0, other arithmetic: 2.33 us -> none  [shards(): return (inv_panel, inv_upper, diag_inv - term)]
    pallas_call x1, Pallas kernels: 75.9 us -> 74.9 us  [shards(): pl.pallas_call(functools.partial(kernel, R, C), out_shape=(jax.ShapeDtype...]
    unnamed x10 -> x5, local copies, waits for them, and re-layouts: 4.72 us -> 4.4 us
where the time goes in v2:
time: 80.1 us; the launch traced here: 79.9 us
  Pallas kernels  74.9 us (94%)
  local copies, waits for them, and re-layouts  4.4 us (5%)
    pallas_call x1, Pallas kernels, shards(): pl.pallas_call(functools.partial(kernel, R, C), out_shape=(jax.ShapeDtype...  74.9 us
    unnamed x5, local copies, waits for them, and re-layouts  4.4 us

profile of v2, /device:TPU:19, one launch (start us, length us, event | category | flops | bytes accessed | tf_op | source)
XLA Modules:
  0.0 79.9 jit_solution(13907335166728557147)
XLA Ops:
  0.6 74.9 %shard_map.76 = (f32[64,1024]{1,0:T(8,128)}, f32[128,512]{1,0:T(8,128)}, f32[4,256,256]{2,1,0:T(8,128)}) custom-call(s32[4,4]{1,0:T(4,128)} %an_hbm.1, s32[8]{0:T(128)} %om_hbm.1, f32[512,256]{1,0:T(8,128)} %t_hbm.1, f32[512,128]{1,0:T(8,128)} %p_ref.1, f32[4,256,256]{2,1,0:T(8,128)} %inv_hbm.1), custom_call_target="tpu_custom_call" | custom-call | tf_op jit(solution)/shard_map/pallas_call | solution.py:314
  75.5 0.0 copy-start
  75.5 1.8 %copy.11 = f32[64,1024]{1,0:T(8,128)} copy(f32[64,1024]{1,0:T(8,128)} %get-tuple-element.6) | data formatting | bytes 524288
  77.3 1.7 %copy.12 = f32[128,512]{1,0:T(8,128)} copy(f32[128,512]{1,0:T(8,128)} %get-tuple-element.7) | data formatting | bytes 524288
  78.9 0.0 copy-done
  78.9 1.0 %copy.13 = f32[4,256,256]{2,1,0:T(8,128)} copy(f32[4,256,256]{2,1,0:T(8,128)S(1)} %copy-done) | data formatting | bytes 2097152
Async XLA Ops:
  75.5 3.4 %copy-start = (f32[4,256,256]{2,1,0:T(8,128)S(1)}, f32[4,256,256]{2,1,0:T(8,128)}, u32[]{:S(2)}) copy-start(f32[4,256,256]{2,1,0:T(8,128)} %get-tuple-element.8) | copy-start | bytes 3145732

commit v3 on v2

--- a/solution.py
+++ b/solution.py
@@ -86,6 +86,21 @@
     for op in loads:
         op.start()
 
+    barrier = pltpu.get_barrier_semaphore()
+
+    @pl.loop(1, R * C)
+    def _(step):
+        peer = lax.rem(r * C + c + step, R * C)
+        pl.semaphore_signal(
+            barrier, inc=1, device_id=(peer // C, lax.rem(peer, C)),
+            device_id_type=pl.DeviceIdType.MESH,
+        )
+
+    for op in loads[:4]:
+        op.wait()
+    t_high[...], t_low[...] = split(t_ref[...])
+    pl.semaphore_wait(barrier, R * C - 1)
+
     own = []
     for step in [*range(1, R), 0]:
         k = lax.rem(r + step, R)
@@ -104,14 +119,10 @@
         @pl.when(dest != c)
         def _():
             copy(*args).start()
-    loads[0].wait()
     for dest, args, span in own:
         @pl.when(dest == c)
         def _():
             pg[r, c] = grp[member, span, :]
-    for op in loads[1:4]:
-        op.wait()
-    t_high[...], t_low[...] = split(t_ref[...])
 
     slots = [[om[an[j, a]] for a in range(an.shape[1])] for j in range(SIBS)]
 
@@ -134,7 +145,9 @@
         return out
 
     row_blocks = rows // NB
-    row_places = [places(r * row_blocks + b) for b in range(row_blocks)]
+    first = (c // 2) // (half // row_blocks)
+    blocks = [flip(first, n) for n in range(row_blocks - 1, -1, -1)]
+    row_places = [places(r * row_blocks + b) for b in blocks]
     my_place = places((r * rows + c * part) // NB)
     col_flags = [flag.astype(F32) for flag in members(c)]
 
@@ -167,6 +180,7 @@
             block = pg.at[source, pl.ds(j * group, group)]
             arrived(block, a2f_s.at[to - 1, j], a2f_r.at[to - 1, j])
 
+    order = [flip(c // 2, step) for step in (*range(half - 1, 0, -1), 0)]
     for s in range(row_blocks):
         for k in range(SHARE):
             scale = [row_places[s][k][j] * col_flags[j] for j in range(SIBS)]
@@ -177,13 +191,12 @@
                         total = total + scale[j] * pg[q, j * group + i]
                     b_ref[s, q * quarter:(q + 1) * quarter,
                           k * NB + i * width:k * NB + (i + 1) * width] = total
-        here = slice(s * NB, (s + 1) * NB)
+        here = pl.ds(pl.multiple_of(blocks[s] * NB, NB), NB)
         y[here, :] = dot3((t_high[here, :], t_low[here, :]), split(b_ref[s]))
-
-    order = [flip(c // 2, step) for step in (*range(half - 1, 0, -1), 0)]
-    for i in order:
-        piece = y.at[pl.ds(pl.multiple_of((2 * i + 1 - par) * part, part), part)]
-        send(piece, yr.at[i], y_s.at[i], y_r.at[i], r, other_c)
+        each = half // row_blocks
+        for i in order[s * each:(s + 1) * each]:
+            piece = y.at[pl.ds(pl.multiple_of((2 * i + 1 - par) * part, part), part)]
+            send(piece, yr.at[i], y_s.at[i], y_r.at[i], r, other_c)
     for step, i in zip((*range(half - 1, 0, -1), 0), order):
         place = pl.ds(pl.multiple_of((2 * i + par) * part, part), part)
         arrived(yr.at[i], y_s.at[i], y_r.at[i])
@@ -204,7 +217,6 @@
         total = total + zr[step - 1]
     for j in range(SIBS):
         block = -(my_place[0][j] * total[:, :NB] + my_place[1][j] * total[:, NB:])
-        panel_ref[:, j * NB:(j + 1) * NB] = block
         for i in range(group):
             stage[j * group + i] = block[:, i * width:(i + 1) * width]
 
@@ -212,17 +224,19 @@
         to = lax.rem(c + step, C)
         send(stage.at[to], u.at[c], u_s.at[step - 1], u_r.at[step - 1], r, to)
     u[c] = stage[c]
+    for j in range(C):
+        panel_ref[:, j * width:(j + 1) * width] = stage[j]
     for step in range(1, C):
         source = lax.rem(c + C - step, C)
         arrived(u.at[source], u_s.at[step - 1], u_r.at[step - 1])
     x = u[...].reshape(rows, width)
-    upper_ref[...] = x.T
 
     d_ref[...] = dot3(mt_split, split(x))
     for step in range(1, R):
         to = lax.rem(r + step, R)
         piece = d_ref.at[pl.ds(pl.multiple_of(to * chunk, chunk), chunk)]
         send(piece, rr.at[step - 1], d_s.at[step - 1], d_r.at[step - 1], to, c)
+    upper_ref[...] = x.T
     total = d_ref[pl.ds(pl.multiple_of(r * chunk, chunk), chunk), :]
     for step in range(1, R):
         arrived(rr.at[step - 1], d_s.at[step - 1], d_r.at[step - 1])
@@ -268,18 +282,24 @@
         before = (which, step)
     onward(*before, par if before[0] == 0 else 1 - par, flip(place, before[1]))
     loads[4].wait()
+
+    def assemble(parity):
+        for column in range(C):
+            j, i = column // group, column % group
+            lanes = slice(i * width, (i + 1) * width)
+            for pair in range(pairs):
+                k = 2 * pair + parity
+                span = pl.ds(pl.multiple_of(k * chunk, chunk), chunk)
+                diag_ref[j, span, lanes] = inv_ref[j, span, lanes] - eg[column % 2, k, column // 2]
+
+    assemble(rpar)
     for which in range(2):
         side = par if which == 0 else 1 - par
         for step in range(half):
             for to in range(pairs):
                 block = eg.at[side, same_parity(other_r, pairs, (pairs - to) % pairs), flip(place, step)]
                 arrived(block, ec_s.at[which, to, step], ec_r.at[which, to, step])
-    for column in range(C):
-        j, i = column // group, column % group
-        lanes = slice(i * width, (i + 1) * width)
-        for k in range(R):
-            span = slice(k * chunk, (k + 1) * chunk)
-            diag_ref[j, span, lanes] = inv_ref[j, span, lanes] - eg[column % 2, k, column // 2]
+    assemble(1 - rpar)
 
     for op in sends:
         op.wait_send()
@@ -342,7 +362,7 @@
             *sems,
         ],
         compiler_params=pltpu.CompilerParams(
-            has_side_effects=True, vmem_limit_bytes=56 * 1024 * 1024
+            has_side_effects=True, vmem_limit_bytes=56 * 1024 * 1024, collective_id=0
         ),
     )(ancestors, owner_map, trailing, panels, diag_inv)
 

time: 80.1 us -> 78 us (0.974)
  Pallas kernels: 74.9 us -> 72.8 us
    pallas_call x1, Pallas kernels: 74.9 us -> 72.8 us  [shards(): pl.pallas_call(functools.partial(kernel, R, C), out_shape=(jax.ShapeDtype...]
where the time goes in v3:
time: 78 us; the launch traced here: 77.8 us
  Pallas kernels  72.8 us (93%)
  local copies, waits for them, and re-layouts  4.4 us (6%)
    pallas_call x1, Pallas kernels, shards(): pl.pallas_call(functools.partial(kernel, R, C), out_shape=(jax.ShapeDtype...  72.8 us
    unnamed x5, local copies, waits for them, and re-layouts  4.4 us

profile of v3, /device:TPU:19, one launch (start us, length us, event | category | flops | bytes accessed | tf_op | source)
XLA Modules:
  0.0 77.8 jit_solution(3538867253644533670)
XLA Ops:
  0.6 72.8 %shard_map.76 = (f32[64,1024]{1,0:T(8,128)}, f32[128,512]{1,0:T(8,128)}, f32[4,256,256]{2,1,0:T(8,128)}) custom-call(s32[4,4]{1,0:T(4,128)} %an_hbm.1, s32[8]{0:T(128)} %om_hbm.1, f32[512,256]{1,0:T(8,128)} %t_hbm.1, f32[512,128]{1,0:T(8,128)} %p_ref.1, f32[4,256,256]{2,1,0:T(8,128)} %inv_hbm.1), custom_call_target="tpu_custom_call" | custom-call | tf_op jit(solution)/shard_map/pallas_call | solution.py:334
  73.4 0.0 copy-start
  73.4 1.8 %copy.11 = f32[64,1024]{1,0:T(8,128)} copy(f32[64,1024]{1,0:T(8,128)} %get-tuple-element.6) | data formatting | bytes 524288
  75.2 1.7 %copy.12 = f32[128,512]{1,0:T(8,128)} copy(f32[128,512]{1,0:T(8,128)} %get-tuple-element.7) | data formatting | bytes 524288
  76.9 0.0 copy-done
  76.9 1.0 %copy.13 = f32[4,256,256]{2,1,0:T(8,128)} copy(f32[4,256,256]{2,1,0:T(8,128)S(1)} %copy-done) | data formatting | bytes 2097152
Async XLA Ops:
  73.4 3.4 %copy-start = (f32[4,256,256]{2,1,0:T(8,128)S(1)}, f32[4,256,256]{2,1,0:T(8,128)}, u32[]{:S(2)}) copy-start(f32[4,256,256]{2,1,0:T(8,128)} %get-tuple-element.8) | copy-start | bytes 3145732

commit v4 on v3

--- a/solution.py
+++ b/solution.py
@@ -197,12 +197,29 @@
         for i in order[s * each:(s + 1) * each]:
             piece = y.at[pl.ds(pl.multiple_of((2 * i + 1 - par) * part, part), part)]
             send(piece, yr.at[i], y_s.at[i], y_r.at[i], r, other_c)
-    for step, i in zip((*range(half - 1, 0, -1), 0), order):
-        place = pl.ds(pl.multiple_of((2 * i + par) * part, part), part)
-        arrived(yr.at[i], y_s.at[i], y_r.at[i])
-        y[place, :] = y[place, :] + yr[i]
-        if step:
-            send(y.at[place], zr.at[step - 1], z_s.at[step - 1], z_r.at[step - 1], r, 2 * i + par)
+    levels = C.bit_length() - 1
+
+    def landing(level, slot):
+        if level == 0:
+            i = flip(c // 2, slot)
+            return yr.at[i], y_s.at[i], y_r.at[i]
+        at = half - (half >> (level - 1)) + slot
+        return zr.at[at], z_s.at[at], z_r.at[at]
+
+    def summed(away, level):
+        place = pl.ds(pl.multiple_of(flip(c, away) * part, part), part)
+        total = y[place, :]
+        for n in range(level):
+            got = landing(n, away >> (n + 1))
+            arrived(*got)
+            total = total + got[0][...]
+        return place, total
+
+    for away in range(C - 2, 0, -2):
+        level = (away & -away).bit_length() - 1
+        place, total = summed(away, level)
+        y[place, :] = total
+        send(y.at[place], *landing(level, away >> (level + 1)), r, flip(c, 1 << level))
 
     for step in range(1, group):
         source = base + lax.rem(member + group - step, group)
@@ -211,10 +228,7 @@
         mt[i * width:(i + 1) * width, :] = grp[i].T
     mt_split = split(mt[...])
 
-    total = y[pl.ds(pl.multiple_of(c * part, part), part), :]
-    for step in range(1, half):
-        arrived(zr.at[step - 1], z_s.at[step - 1], z_r.at[step - 1])
-        total = total + zr[step - 1]
+    _, total = summed(0, levels)
     for j in range(SIBS):
         block = -(my_place[0][j] * total[:, :NB] + my_place[1][j] * total[:, NB:])
         for i in range(group):

time: 78 us -> 79.3 us (1.017)
  Pallas kernels: 72.8 us -> 74 us
    pallas_call x1, Pallas kernels: 72.8 us -> 74 us  [shards(): pl.pallas_call(functools.partial(kernel, R, C), out_shape=(jax.ShapeDtype...]
where the time goes in v4:
time: 79.3 us; the launch traced here: 79.1 us
  Pallas kernels  74 us (93%)
  local copies, waits for them, and re-layouts  4.4 us (6%)
    pallas_call x1, Pallas kernels, shards(): pl.pallas_call(functools.partial(kernel, R, C), out_shape=(jax.ShapeDtype...  74 us
    unnamed x5, local copies, waits for them, and re-layouts  4.4 us

profile of v4, /device:TPU:19, one launch (start us, length us, event | category | flops | bytes accessed | tf_op | source)
XLA Modules:
  0.0 79.1 jit_solution(14293205153367029893)
XLA Ops:
  0.6 74.0 %shard_map.76 = (f32[64,1024]{1,0:T(8,128)}, f32[128,512]{1,0:T(8,128)}, f32[4,256,256]{2,1,0:T(8,128)}) custom-call(s32[4,4]{1,0:T(4,128)} %an_hbm.1, s32[8]{0:T(128)} %om_hbm.1, f32[512,256]{1,0:T(8,128)} %t_hbm.1, f32[512,128]{1,0:T(8,128)} %p_ref.1, f32[4,256,256]{2,1,0:T(8,128)} %inv_hbm.1), custom_call_target="tpu_custom_call" | custom-call | tf_op jit(solution)/shard_map/pallas_call | solution.py:348
  74.7 0.0 copy-start
  74.7 1.8 %copy.11 = f32[64,1024]{1,0:T(8,128)} copy(f32[64,1024]{1,0:T(8,128)} %get-tuple-element.6) | data formatting | bytes 524288
  76.4 1.7 %copy.12 = f32[128,512]{1,0:T(8,128)} copy(f32[128,512]{1,0:T(8,128)} %get-tuple-element.7) | data formatting | bytes 524288
  78.1 0.0 copy-done
  78.1 1.0 %copy.13 = f32[4,256,256]{2,1,0:T(8,128)} copy(f32[4,256,256]{2,1,0:T(8,128)S(1)} %copy-done) | data formatting | bytes 2097152
Async XLA Ops:
  74.7 3.4 %copy-start = (f32[4,256,256]{2,1,0:T(8,128)S(1)}, f32[4,256,256]{2,1,0:T(8,128)}, u32[]{:S(2)}) copy-start(f32[4,256,256]{2,1,0:T(8,128)} %get-tuple-element.8) | copy-start | bytes 3145732
